TPU v7x, 32 devices: a whole 2x2x4 slice. The times are simulated.
32 devices in a mesh: grp: 4 (over z), sub: 8 (over y, x, core).
Axes of the slice: x: 2, y: 2, z: 4, core: 2. Of those that a mesh axis runs over, the one named last changes fastest.
Arguments:
- columns: bfloat16 [8, 65536, 512], P('grp', 'sub'), may hold values from -6 to 6
- in_basis: bfloat16 [8, 65536, 128], P('grp', 'sub'), may hold values from -0.375 to 0.375
- out_basis: bfloat16 [8, 65536, 128], P('grp', 'sub'), may hold values from -0.5 to 0.5
- transfer: bfloat16 [8, 8, 256, 2, 128, 128], P('grp', None, 'sub'), may hold values from -0.375 to 0.375
- true_ranks: int32 [8, 9, 256], P('grp', None, 'sub'), may hold values from 96 to 128
- target: bfloat16 [65536, 512], P('sub'), may hold values from -9 to 9
Outputs:
- gradient: bfloat16 [8, 65536, 512], P('grp', 'sub')
- residual: bfloat16 [65536, 512], P('sub')
Inputs may be any that keep to these rules, and one draw needn't show every extreme that they name: true_ranks[g, l, j] is the number of leading rows of block [g, j] that carry data after level l; the remaining rows of the 128 are padding.
All inputs are finite; a program needn't handle non-finite values.
Results may differ from a plain program's by a relative error of at most 0.025.
Values may be sent and summed in bfloat16 or wider, within the bound.
A program may use at most 192 MiB of HBM per device.

v0:
```python
import jax
import jax.numpy as jnp
from jax import lax
from jax.sharding import PartitionSpec as P


def partner_2(shard, axis, bit):
    return lax.ppermute(shard, axis, [(i, i ^ 1 << bit) for i in range(lax.axis_size(axis))])


def masked(values, rank_rows):
    lane_ids = lax.broadcasted_iota(jnp.int32, (1, 1, values.shape[2], 1), 2)
    return jnp.where(lane_ids < rank_rows[:, :, None, None], values, 0.0).astype(jnp.bfloat16)


def local_partner(values, stride):
    groups = values.shape[0]
    blocks = values.shape[1]
    shaped = values.reshape(
        groups, blocks // (2 * stride), 2, stride, values.shape[2], values.shape[3]
    )
    return jnp.flip(shaped, axis=2).reshape(values.shape)


def body(columns, in_basis, out_basis, transfer, true_ranks, target):
    groups = columns.shape[0]
    row_count = columns.shape[1]
    rhs_count = columns.shape[2]
    rank_width = in_basis.shape[2]
    levels = transfer.shape[1]
    blocks = transfer.shape[2]
    leaf_rows = row_count // blocks
    local_levels = blocks.bit_length() - 1
    in_leaves = in_basis.reshape(groups, blocks, leaf_rows, rank_width)
    out_leaves = out_basis.reshape(groups, blocks, leaf_rows, rank_width)
    column_leaves = columns.reshape(groups, blocks, leaf_rows, rhs_count)
    carried = masked(
        jnp.einsum("gjbr,gjbn->gjrn", in_leaves, column_leaves, preferred_element_type=jnp.float32),
        true_ranks[:, 0],
    )
    for step_index in range(levels):
        stride = 1 << step_index
        if stride < blocks:
            partner = local_partner(carried, stride)
        else:
            partner = partner_2(carried, "sub", step_index - local_levels)
        combined = jnp.einsum(
            "gjrq,gjqn->gjrn",
            transfer[:, step_index, :, 0],
            carried,
            preferred_element_type=jnp.float32,
        )
        combined = combined + jnp.einsum(
            "gjrq,gjqn->gjrn",
            transfer[:, step_index, :, 1],
            partner,
            preferred_element_type=jnp.float32,
        )
        carried = masked(combined, true_ranks[:, step_index + 1])
    images = jnp.einsum("gjbr,gjrn->gjbn", out_leaves, carried, preferred_element_type=jnp.float32)
    partial_value = jnp.sum(images.reshape(groups, row_count, rhs_count), axis=0)
    summed = lax.psum(partial_value.astype(jnp.bfloat16), "grp").astype(jnp.float32)
    residual = (summed - target.astype(jnp.float32)).astype(jnp.bfloat16)
    residual_leaves = residual.reshape(blocks, leaf_rows, rhs_count)
    cotangent = masked(
        jnp.einsum(
            "gjbr,jbn->gjrn", out_leaves, residual_leaves, preferred_element_type=jnp.float32
        ),
        true_ranks[:, levels],
    )
    for step_index in reversed(range(levels)):
        stride = 1 << step_index
        direct = jnp.einsum(
            "gjqr,gjqn->gjrn",
            transfer[:, step_index, :, 0],
            cotangent,
            preferred_element_type=jnp.float32,
        )
        across = jnp.einsum(
            "gjqr,gjqn->gjrn",
            transfer[:, step_index, :, 1],
            cotangent,
            preferred_element_type=jnp.float32,
        ).astype(jnp.bfloat16)
        if stride < blocks:
            arriving = local_partner(lax.optimization_barrier(across), stride)
        else:
            arriving = partner_2(across, "sub", step_index - local_levels)
        cotangent = masked(direct + arriving.astype(jnp.float32), true_ranks[:, step_index])
    gradient = jnp.einsum(
        "gjbr,gjrn->gjbn", in_leaves, cotangent, preferred_element_type=jnp.float32
    )
    gradient = gradient.astype(jnp.bfloat16).reshape(groups, row_count, rhs_count)
    return (gradient, residual)


def solution(mesh):
    return jax.shard_map(
        body,
        mesh=mesh,
        in_specs=(
            P("grp", "sub", None),
            P("grp", "sub", None),
            P("grp", "sub", None),
            P("grp", None, "sub", None, None, None),
            P("grp", None, "sub"),
            P("sub", None),
        ),
        out_specs=(P("grp", "sub", None), P("sub", None)),
        check_vma=False,
    )
```

profile of v0, /device:TPU:0, one launch (start us, length us, event | category | flops | bytes accessed | tf_op | source)
XLA Modules:
  0.0 1561.6 jit_solution(11016867688535052051)
XLA Ops:
  28.0 12.5 fusion.68
  40.5 14.2 select_convert_fusion.7
  54.7 12.5 fusion.62
  74.9 13.8 select_convert_fusion.6
  88.8 12.5 fusion.57
  108.9 13.7 select_convert_fusion.5
  122.5 12.5 fusion.52
  142.8 13.7 select_convert_fusion.4
  156.4 12.5 fusion.47
  176.6 13.9 select_convert_fusion.3
  190.9 12.5 fusion.42
  204.0 13.7 select_convert_fusion.2
  220.6 12.5 fusion.37
  233.1 168.5 %collective-permute-done.1 = bf16[2,32,128,512]{2,3,1,0:T(8,128)(2,1)} collective-permute-done((bf16[2,32,128,512]{2,3,1,0:T(8,128)(2,1)}, bf16[2,32,128,512]{2,3,1,0:T(8,128)(2,1)}, u32[]{:S(2)}, u32[]{:S(2)}) %collective-permute-start.1) | collective-permute-done | bytes 8388640 | tf_op jit(solution)/shard_map/ppermute | solution.py:8
  401.6 13.7 select_convert_fusion.1
  417.1 12.5 fusion.32
  429.6 167.9 %collective-permute-done.2 = bf16[2,32,128,512]{2,3,1,0:T(8,128)(2,1)} collective-permute-done((bf16[2,32,128,512]{2,3,1,0:T(8,128)(2,1)}, bf16[2,32,128,512]{2,3,1,0:T(8,128)(2,1)}, u32[]{:S(2)}, u32[]{:S(2)}) %collective-permute-start.2) | collective-permute-done | bytes 8388640 | tf_op jit(solution)/shard_map/ppermute | solution.py:8
  597.5 15.1 bitcast_convert_fusion
  612.7 292.2 %all-reduce.2.cloned.1.call-done = bf16[8192,512]{1,0:T(8,128)(2,1)} async-done(((bf16[8192,512]{1,0:T(8,128)(2,1)}), bf16[8192,512]{1,0:T(8,128)(2,1)}) %all-reduce.2.cloned.1.call-update) | async-done | bytes 8388624 | tf_op jit(solution)/shard_map/psum | solution.py:62
  930.8 180.8 %collective-permute-done.3 = bf16[2,32,128,512]{3,2,1,0:T(8,128)(2,1)} collective-permute-done((bf16[2,32,128,512]{3,2,1,0:T(8,128)(2,1)S(1)}, bf16[2,32,128,512]{3,2,1,0:T(8,128)(2,1)}, u32[]{:S(2)}, u32[]{:S(2)}) %collective-permute-start.3) | collective-permute-done | bytes 8388640 | tf_op jit(solution)/shard_map/ppermute | solution.py:8
  1128.8 180.0 %collective-permute-done.4 = bf16[2,32,128,512]{3,2,1,0:T(8,128)(2,1)} collective-permute-done((bf16[2,32,128,512]{3,2,1,0:T(8,128)(2,1)S(1)}, bf16[2,32,128,512]{3,2,1,0:T(8,128)(2,1)}, u32[]{:S(2)}, u32[]{:S(2)}) %collective-permute-start.4) | collective-permute-done | bytes 8388640 | tf_op jit(solution)/shard_map/ppermute | solution.py:8
  1324.6 13.3 collective-permute-done.5
  1436.3 13.2 copy.55
  1536.3 18.0 %convolution_convert_fusion = bf16[2,32,512,256]{2,3,1,0:T(8,128)(2,1)} fusion(bf16[2,32,256,128]{3,2,1,0:T(8,128)(2,1)} %bitcast.282, bf16[2,32,128,512]{3,2,1,0:T(8,128)(2,1)} %bitcast.278, pred[2,32,128]{2,1,0:T(8,128)(4,1)S(1)} %copy-done.1, bf16[2,32,128,512]{3,2,1,0:T(8,128)(2,1)} %fusion.3, bf16[2,8,32,2,128,128]{5,4,3,2,1,0:T(8,128)(2,1)} %param.9), kind=kOutput, calls=%fused_computation.37 | convolution fusion | flops 3246391296 | bytes 39854080 | tf_op jit(solution)/shard_map/gjbr,gjrn->gjbn/dot_general | solution.py:90
  (70 shorter events, 301.4 us)
Async XLA Ops:
  7.2 897.7 %all-reduce.2.cloned.1.call-start = ((), (), s32[]{:S(2)}) async-start(), calls=%async_computation | async-start | bytes 16777216 | tf_op jit(solution)/shard_map/psum | solution.py:62
  8.7 11.6 copy-start
  8.7 31.8 %copy-start.2 = (pred[2,32,128]{2,1,0:T(8,128)(4,1)}, pred[2,32,128]{2,1,0:T(8,128)(4,1)S(1)}, u32[]{:S(2)}) copy-start(pred[2,32,128]{2,1,0:T(8,128)(4,1)S(1)} %get-tuple-element.15) | copy-start | bytes 24580
  74.9 13.9 copy-start.4
  74.9 34.0 %copy-start.6 = (pred[2,32,128]{2,1,0:T(8,128)(4,1)}, pred[2,32,128]{2,1,0:T(8,128)(4,1)S(1)}, u32[]{:S(2)}) copy-start(pred[2,32,128]{2,1,0:T(8,128)(4,1)S(1)} %get-tuple-element.13) | copy-start | bytes 24580
  142.7 13.7 copy-start.8
  190.4 13.6 collective-permute-start
  217.7 183.9 %collective-permute-start.1 = (bf16[2,32,128,512]{2,3,1,0:T(8,128)(2,1)}, bf16[2,32,128,512]{2,3,1,0:T(8,128)(2,1)}, u32[]{:S(2)}, u32[]{:S(2)}) collective-permute-start(bf16[2,32,128,512]{2,3,1,0:T(8,128)(2,1)} %bitcast.286), channel_id=1, source_target_pairs={{0,2},{1,3},{2,0},{3,1},{4,6},{5,7},{6,4},{7,5},{8,10},{9,11},{10,... | collective-permute-start | bytes 25165832 | tf_op jit(solution)/shard_map/ppermute | solution.py:8
  233.1 183.9 %copy-start.10 = (s32[2,32]{1,0:T(2,128)S(1)}, s32[2,32]{1,0:T(2,128)}, u32[]{:S(2)}) copy-start(s32[2,32]{1,0:T(2,128)} %get-tuple-element.10) | copy-start | bytes 772
  415.2 182.3 %collective-permute-start.2 = (bf16[2,32,128,512]{2,3,1,0:T(8,128)(2,1)}, bf16[2,32,128,512]{2,3,1,0:T(8,128)(2,1)}, u32[]{:S(2)}, u32[]{:S(2)}) collective-permute-start(bf16[2,32,128,512]{2,3,1,0:T(8,128)(2,1)} %bitcast.284), channel_id=1, source_target_pairs={{0,4},{1,5},{2,6},{3,7},{4,0},{5,1},{6,2},{7,3},{8,12},{9,13},{10,... | collective-permute-start | bytes 25165832 | tf_op jit(solution)/shard_map/ppermute | solution.py:8
  929.2 182.4 %collective-permute-start.3 = (bf16[2,32,128,512]{3,2,1,0:T(8,128)(2,1)S(1)}, bf16[2,32,128,512]{3,2,1,0:T(8,128)(2,1)}, u32[]{:S(2)}, u32[]{:S(2)}) collective-permute-start(bf16[2,32,128,512]{3,2,1,0:T(8,128)(2,1)S(1)} %convert_bitcast_fusion.7), channel_id=1, source_target_pairs={{0,4},{1,5},{2,6},{3,7},{4,0},{5,1},{6,2},{7,3},{8,12},{9,13},{10,... | collective-permute-start | bytes 25165832 | tf_op jit(solution)/shard_map/ppermute | solution.py:8
  1127.3 181.5 %collective-permute-start.4 = (bf16[2,32,128,512]{3,2,1,0:T(8,128)(2,1)S(1)}, bf16[2,32,128,512]{3,2,1,0:T(8,128)(2,1)}, u32[]{:S(2)}, u32[]{:S(2)}) collective-permute-start(bf16[2,32,128,512]{3,2,1,0:T(8,128)(2,1)S(1)} %convert_bitcast_fusion.6), channel_id=1, source_target_pairs={{0,2},{1,3},{2,0},{3,1},{4,6},{5,7},{6,4},{7,5},{8,10},{9,11},{10,... | collective-permute-start | bytes 25165832 | tf_op jit(solution)/shard_map/ppermute | solution.py:8
  1324.6 13.4 collective-permute-start.5
  1369.5 7.8 copy-start.9
  1408.5 7.6 copy-start.7
  1449.6 7.8 copy-start.5
  1488.9 7.6 copy-start.3
  1528.7 7.6 copy-start.1
Sparse Core Ops, SparseCore 0:
  612.8 292.0 all-reduce.1
where the time goes:
time: 1570 us; the launch traced here: 1560 us
  waiting for transfers between devices  1000 us (64%)
  matrix products  388 us (25%)
  local copies, waits for them, and re-layouts  138 us (9%)
    ppermute x6, waiting for transfers between devices, partner_2(): lax.ppermute(shard, axis, [(i, i ^ 1 << bit) for i in range(lax.axis_size...  711 us
    psum x1, waiting for transfers between devices, body(): lax.psum(partial_value.astype(jnp.bfloat16), 'grp').astype(jnp.float32)  292 us
    dot_general x8, matrix products, body(): jnp.einsum('gjrq,gjqn->gjrn', transfer[:, step_index, :, 0], carried, pre...  100 us
    dot_general x7, matrix products, body(): jnp.einsum('gjrq,gjqn->gjrn', transfer[:, step_index, :, 1], partner, pre...  96.5 us
    rev x10, local copies, waits for them, and re-layouts, local_partner(): return jnp.flip(shaped, axis=2).reshape(values.shape)  76.5 us
    dot_general x7, matrix products, body(): jnp.einsum('gjqr,gjqn->gjrn', transfer[:, step_index, :, 0], cotangent, p...  72.1 us
    dot_general x8, matrix products, body(): jnp.einsum('gjqr,gjqn->gjrn', transfer[:, step_index, :, 1], cotangent, p...  65.1 us
    reshape x5, local copies, waits for them, and re-layouts, local_partner(): values.reshape(groups, blocks // (2 * stride), 2, stride, values.shape[2]...  59.6 us
  transfers between devices with their start and end apart: 7, of which 7 were waited for; matrix products, arithmetic and copies ran while one was open for 2% of the time, Pallas kernels for 0%

commit v1 on v0

v1 whole, which is shorter than its diff:
```python
import functools

import jax
import jax.numpy as jnp
from jax import lax
from jax.experimental import pallas as pl
from jax.experimental.pallas import tpu as pltpu
from jax.sharding import PartitionSpec as P

F32 = jnp.float32
BF16 = jnp.bfloat16
VMEM_LIMIT = 54 * 1024 * 1024
COLUMN_PARTS = 2
BLOCK_PARTS = 4


def partner_of(shard, bit):
    return lax.ppermute(shard, "sub", [(i, i ^ 1 << bit) for i in range(lax.axis_size("sub"))])


def dot(a, b):
    return jnp.dot(a, b, preferred_element_type=F32)


def dot_t(a, b):
    return lax.dot_general(a, b, (((0,), (0,)), ((), ())), preferred_element_type=F32)


def keep(values, rank):
    rows = lax.broadcasted_iota(jnp.int32, values.shape, 0)
    return jnp.where(rows < rank, values, 0.0).astype(BF16)


def pair_of(pair, stride):
    low = (pair // stride) * (2 * stride) + pair % stride
    return low, low + stride


def pair_weights(w_ref, level, j, p):
    top = jnp.concatenate([w_ref[0, level, j, 0], w_ref[0, level, j, 1]], axis=1)
    low = jnp.concatenate([w_ref[0, level, p, 1], w_ref[0, level, p, 0]], axis=1)
    return jnp.concatenate([top, low], axis=0)


def start_kernel(local_levels, leaf, ranks, in_ref, col_ref, w_ref, *rest):
    outs, state = rest[:-1], rest[-1]
    g = pl.program_id(0)
    blocks, rank = state.shape[0], state.shape[1]

    def first(j, _):
        rows = pl.ds(pl.multiple_of(j * leaf, leaf), leaf)
        state[j] = keep(dot_t(in_ref[0, rows], col_ref[0, rows]), ranks[g, 0, j])
        return 0

    lax.fori_loop(0, blocks, first, 0, unroll=min(4, blocks))
    for level in range(local_levels):
        def step(pair, _):
            j, p = pair_of(pair, 1 << level)
            both = jnp.concatenate([state[j], state[p]], axis=0)
            made = dot(pair_weights(w_ref, level, j, p), both)
            state[j] = keep(made[:rank], ranks[g, level + 1, j])
            state[p] = keep(made[rank:], ranks[g, level + 1, p])
            return 0

        lax.fori_loop(0, blocks // 2, step, 0, unroll=min(4, blocks // 2))
    part = blocks // len(outs)
    for b, out in enumerate(outs):
        out[0] = state[b * part:(b + 1) * part]


def level_kernel(level, first_block, ranks, s_ref, p_ref, w_ref, out_ref):
    groups, size = s_ref.shape[:2]
    base = first_block + pl.program_id(0) * size
    for g in range(groups):
        for j in range(size):
            both = jnp.concatenate([s_ref[g, j], p_ref[g, j]], axis=0)
            weights = jnp.concatenate([w_ref[g, 0, j, 0], w_ref[g, 0, j, 1]], axis=1)
            out_ref[g, j] = keep(dot(weights, both), ranks[g, level + 1, base + j])


def image_kernel(level, first_block, leaf, ranks, s_ref, p_ref, w_ref, ob_ref, out_ref):
    groups, size = s_ref.shape[:2]
    base = first_block + pl.program_id(0) * size
    for j in range(size):
        rows = slice(j * leaf, (j + 1) * leaf)
        states = []
        for g in range(groups):
            both = jnp.concatenate([s_ref[g, j], p_ref[g, j]], axis=0)
            weights = jnp.concatenate([w_ref[g, 0, j, 0], w_ref[g, 0, j, 1]], axis=1)
            states.append(keep(dot(weights, both), ranks[g, level + 1, base + j]))
        basis = jnp.concatenate([ob_ref[g, rows] for g in range(groups)], axis=1)
        out_ref[rows] = dot(basis, jnp.concatenate(states, axis=0)).astype(BF16)


def residual_kernel(level, first_block, leaf, ranks, sum_ref, target_ref, ob_ref, w_ref, *rest):
    res_ref, back_ref, across_ref = rest[-3:]
    groups, size = back_ref.shape[:2]
    base = first_block + pl.program_id(0) * size
    for j in range(size):
        rows = slice(j * leaf, (j + 1) * leaf)
        residual = (sum_ref[rows].astype(F32) - target_ref[rows].astype(F32)).astype(BF16)
        res_ref[rows] = residual
        for g in range(groups):
            back = keep(dot_t(ob_ref[g, rows], residual), ranks[g, level + 1, base + j])
            back_ref[g, j] = back
            across_ref[g, j] = dot_t(w_ref[g, 0, j, 1], back).astype(BF16)


def back_kernel(level, first_block, ranks, back_ref, arr_ref, w_ref, v_ref, out_ref, across_ref):
    groups, size = back_ref.shape[:2]
    base = first_block + pl.program_id(0) * size
    for g in range(groups):
        for j in range(size):
            made = dot_t(w_ref[g, 0, j, 0], back_ref[g, j]) + arr_ref[g, j].astype(F32)
            back = keep(made, ranks[g, level, base + j])
            out_ref[g, j] = back
            across_ref[g, j] = dot_t(v_ref[g, 0, j, 1], back).astype(BF16)


def end_kernel(local_levels, parts, leaf, ranks, *refs):
    backs, arrs = refs[:parts], refs[parts:2 * parts]
    w_ref, in_ref = refs[2 * parts:2 * parts + 2]
    grad_ref, state = refs[-2:]
    g = pl.program_id(0)
    blocks, rank = state.shape[0], state.shape[1]
    part = blocks // parts
    for b in range(parts):
        def enter(k, _):
            j = b * part + k
            made = dot_t(w_ref[0, local_levels, j, 0], backs[b][0, k]) + arrs[b][0, k].astype(F32)
            state[j] = keep(made, ranks[g, local_levels, j])
            return 0

        lax.fori_loop(0, part, enter, 0, unroll=min(4, part))
    for level in reversed(range(local_levels)):
        def step(pair, _):
            j, p = pair_of(pair, 1 << level)
            both = jnp.concatenate([state[j], state[p]], axis=0)
            made = dot_t(pair_weights(w_ref, level, j, p), both)
            state[j] = keep(made[:rank], ranks[g, level, j])
            state[p] = keep(made[rank:], ranks[g, level, p])
            return 0

        lax.fori_loop(0, blocks // 2, step, 0, unroll=min(4, blocks // 2))

    def last(j, _):
        rows = pl.ds(pl.multiple_of(j * leaf, leaf), leaf)
        grad_ref[0, rows] = dot(in_ref[0, rows], state[j]).astype(BF16)
        return 0

    lax.fori_loop(0, blocks, last, 0, unroll=min(4, blocks))


def body(columns, in_basis, out_basis, transfer, true_ranks, target):
    groups, row_count, rhs = columns.shape
    rank = in_basis.shape[2]
    levels, blocks = transfer.shape[1], transfer.shape[2]
    leaf = row_count // blocks
    local_levels = blocks.bit_length() - 1
    width = rhs // COLUMN_PARTS
    parts = min(BLOCK_PARTS, blocks)
    part = blocks // parts
    size = min(4, part)
    steps = part // size

    def call(kernel, grid, in_specs, out_specs, out_shape, operands, flops, scratch=(), alias=None):
        nbytes = 2 * sum(o.size for o in jax.tree.leaves(out_shape))
        nbytes += flops // 256
        return pl.pallas_call(
            kernel,
            grid_spec=pltpu.PrefetchScalarGridSpec(
                num_scalar_prefetch=1, grid=(grid,), in_specs=in_specs, out_specs=out_specs,
                scratch_shapes=scratch,
            ),
            out_shape=out_shape,
            input_output_aliases=alias or {},
            cost_estimate=pl.CostEstimate(flops=flops, bytes_accessed=nbytes, transcendentals=0),
            compiler_params=pltpu.CompilerParams(vmem_limit_bytes=VMEM_LIMIT),
        )(true_ranks, *operands)

    chunk = jax.ShapeDtypeStruct((groups, part, rank, width), BF16)
    chunk_spec = pl.BlockSpec((groups, size, rank, width), lambda i, r: (0, i, 0, 0))
    group_spec = pl.BlockSpec((1, part, rank, width), lambda g, r: (g, 0, 0, 0))
    any_spec = pl.BlockSpec(memory_space=pl.ANY)
    unit = 2 * groups * part * rank * rank * width

    def level_spec(level, b):
        return pl.BlockSpec(
            (groups, 1, size, 2, rank, rank), lambda i, r: (0, level, b * steps + i, 0, 0, 0)
        )

    def local_spec(count):
        return pl.BlockSpec(
            (1, count, blocks, 2, rank, rank), lambda g, r: (g, 0, 0, 0, 0, 0)
        )

    def basis_spec(b):
        return pl.BlockSpec((groups, size * leaf, rank), lambda i, r: (0, b * steps + i, 0))

    def start(c):
        return call(
            functools.partial(start_kernel, local_levels, leaf),
            groups,
            [
                pl.BlockSpec((1, row_count, rank), lambda g, r: (g, 0, 0)),
                pl.BlockSpec((1, row_count, width), lambda g, r: (g, 0, c)),
                local_spec(local_levels),
            ],
            [group_spec] * parts,
            [chunk] * parts,
            (in_basis, columns, transfer),
            unit * parts * 2 * (local_levels + 1),
            scratch=[pltpu.VMEM((blocks, rank, width), BF16)],
        )

    def forward(level, b, s):
        p = partner_of(s, level - local_levels)
        if level < levels - 1:
            return call(
                functools.partial(level_kernel, level, b * part),
                steps,
                [chunk_spec, chunk_spec, level_spec(level, b)],
                chunk_spec,
                chunk,
                (s, p, transfer),
                unit * 2,
            )
        return call(
            functools.partial(image_kernel, level, b * part, leaf),
            steps,
            [chunk_spec, chunk_spec, level_spec(level, b), basis_spec(b)],
            pl.BlockSpec((size * leaf, width), lambda i, r: (i, 0)),
            jax.ShapeDtypeStruct((part * leaf, width), BF16),
            (s, p, transfer, out_basis),
            unit * 4,
        )

    def at_residual(c, b, summed, residual):
        row_spec = pl.BlockSpec((size * leaf, width), lambda i, r: (b * steps + i, c))
        operands = [summed, target, out_basis, transfer]
        specs = [
            pl.BlockSpec((size * leaf, width), lambda i, r: (i, 0)),
            row_spec,
            basis_spec(b),
            level_spec(levels - 1, b),
        ]
        if residual is not None:
            operands.append(residual)
            specs.append(any_spec)
        return call(
            functools.partial(residual_kernel, levels - 1, b * part, leaf),
            steps,
            specs,
            [row_spec, chunk_spec, chunk_spec],
            [jax.ShapeDtypeStruct((row_count, rhs), BF16), chunk, chunk],
            operands,
            unit * 3,
            alias={5: 0} if residual is not None else None,
        )

    def backward(level, b, back, arriving):
        return call(
            functools.partial(back_kernel, level, b * part),
            steps,
            [chunk_spec, chunk_spec, level_spec(level, b), level_spec(level - 1, b)],
            [chunk_spec, chunk_spec],
            [chunk, chunk],
            (back, arriving, transfer, transfer),
            unit * 2,
        )

    def end(c, backs, arrs, gradient):
        operands = [*backs, *arrs, transfer, in_basis]
        specs = [group_spec] * (2 * parts) + [
            local_spec(local_levels + 1),
            pl.BlockSpec((1, row_count, rank), lambda g, r: (g, 0, 0)),
        ]
        if gradient is not None:
            operands.append(gradient)
            specs.append(any_spec)
        return call(
            functools.partial(end_kernel, local_levels, parts, leaf),
            groups,
            specs,
            pl.BlockSpec((1, row_count, width), lambda g, r: (g, 0, c)),
            jax.ShapeDtypeStruct((groups, row_count, rhs), BF16),
            operands,
            unit * parts * 2 * (local_levels + 1),
            scratch=[pltpu.VMEM((blocks, rank, width), BF16)],
            alias={len(operands): 0} if gradient is not None else None,
        )

    residual = None
    gradient = None
    kept = {}
    previous = None
    for c in range(COLUMN_PARTS):
        states = start(c)
        for b in range(parts):
            s = states[b]
            for level in range(local_levels, levels):
                s = forward(level, b, s)
            if previous is not None:
                s, previous = lax.optimization_barrier((s, previous))
            previous = lax.psum(s, "grp")
            kept[c, b] = previous
    for c in range(COLUMN_PARTS):
        backs, arrs = [], []
        for b in range(parts):
            residual, back, across = at_residual(c, b, kept[c, b], residual)
            for level in reversed(range(local_levels, levels)):
                arriving = partner_of(across, level - local_levels)
                if level > local_levels:
                    back, across = backward(level, b, back, arriving)
            backs.append(back)
            arrs.append(arriving)
        gradient = end(c, backs, arrs, gradient)
    return gradient, residual


def solution(mesh):
    return jax.shard_map(
        body,
        mesh=mesh,
        in_specs=(
            P("grp", "sub", None),
            P("grp", "sub", None),
            P("grp", "sub", None),
            P("grp", None, "sub", None, None, None),
            P("grp", None, "sub"),
            P("sub", None),
        ),
        out_specs=(P("grp", "sub", None), P("sub", None)),
        check_vma=False,
    )
```

time: 1570 us -> 857 us (0.55)
  waiting for transfers between devices: 1000 us -> 364 us
  Pallas kernels: 0 us -> 400 us
  matrix products: 388 us -> 0 us
  local copies, waits for them, and re-layouts: 138 us -> 21.5 us
  starting transfers between devices: 8.31 us -> 44.2 us
    ppermute x6 -> x48, waiting for transfers between devices: 711 us -> 152 us  [partner_of(): lax.ppermute(shard, 'sub', [(i, i ^ 1 << bit) for i in range(lax.axis_siz...]
    pallas_call x0 -> x52, Pallas kernels: none -> 400 us  [call(): pl.pallas_call(kernel, grid_spec=pltpu.PrefetchScalarGridSpec(num_scalar_...]
    dot_general x34 -> x0, matrix products: 388 us -> none  [the longest x8 100 us: body(): jnp.einsum('gjrq,gjqn->gjrn', transfer[:, step_index, :, 0], carried, pre...]
    psum x1 -> x8, waiting for transfers between devices: 292 us -> 211 us  [body(): previous = lax.psum(s, 'grp')]
    rev x10 -> x0, local copies, waits for them, and re-layouts: 76.5 us -> none  [local_partner(): return jnp.flip(shaped, axis=2).reshape(values.shape)]
    reshape x5 -> x0, local copies, waits for them, and re-layouts: 59.6 us -> none  [local_partner(): values.reshape(groups, blocks // (2 * stride), 2, stride, values.shape[2]...]
    ppermute x6 -> x48, starting transfers between devices: 8.28 us -> 43.5 us  [partner_of(): lax.ppermute(shard, 'sub', [(i, i ^ 1 << bit) for i in range(lax.axis_siz...]
    unnamed x22 -> x83, local copies, waits for them, and re-layouts: 0.04 us -> 21.5 us
  transfers between devices with their start and end apart: 7 -> 56, of which waited for: 7 -> 20; matrix products, arithmetic and copies ran while one was open for 2% -> 0% of each run, Pallas kernels for 0% -> 36%
where the time goes in v1:
time: 857 us; the launch traced here: 844 us
  Pallas kernels  400 us (47%)
  waiting for transfers between devices  364 us (42%)
  starting transfers between devices  44.2 us (5%)
  local copies, waits for them, and re-layouts  21.5 us (3%)
  between operations  14.7 us (2%)
    pallas_call x52, Pallas kernels, call(): pl.pallas_call(kernel, grid_spec=pltpu.PrefetchScalarGridSpec(num_scalar_...  400 us
    psum x8, waiting for transfers between devices, body(): previous = lax.psum(s, 'grp')  211 us
    ppermute x48, waiting for transfers between devices, partner_of(): lax.ppermute(shard, 'sub', [(i, i ^ 1 << bit) for i in range(lax.axis_siz...  152 us
    ppermute x48, starting transfers between devices, partner_of(): lax.ppermute(shard, 'sub', [(i, i ^ 1 << bit) for i in range(lax.axis_siz...  43.5 us
    unnamed x83, local copies, waits for them, and re-layouts  21.5 us
  transfers between devices with their start and end apart: 56, of which 20 were waited for; matrix products, arithmetic and copies ran while one was open for 0% of the time, Pallas kernels for 36%

profile of v1, /device:TPU:0, one launch (start us, length us, event | category | flops | bytes accessed | tf_op | source)
XLA Modules:
  0.0 844.0 jit_solution(16743775836735398772)
XLA Ops:
  8.5 42.9 %shard_map.81 = (bf16[2,8,128,256]{3,2,1,0:T(8,128)(2,1)}, bf16[2,8,128,256]{3,2,1,0:T(8,128)(2,1)}, bf16[2,8,128,256]{3,2,1,0:T(8,128)(2,1)}, bf16[2,8,128,256]{3,2,1,0:T(8,128)(2,1)}) custom-call(s32[2,9,32]{2,1,0:T(8,128)} %copy.67.ranks, bf16[2,8192,128]{2,1,0:T(8,128)(2,1)} %refs_9_.3, bf16[2,8192,512]{2,1,0:T(8,128)(2,1)} %col_ref.3, ...), custom_call_target="tpu_custom_call" | custom-call | flops 6442450944 | bytes 29360128 | tf_op jit(solution)/shard_map/pallas_call | solution.py:169
  67.2 19.0 %collective-permute-done.13.p_ref = bf16[2,8,128,256]{3,2,1,0:T(8,128)(2,1)S(1)} collective-permute-done((bf16[2,8,128,256]{3,2,1,0:T(8,128)(2,1)}, bf16[2,8,128,256]{3,2,1,0:T(8,128)(2,1)S(1)}, u32[]{:S(2)}, u32[]{:S(2)}) %collective-permute-start.13) | collective-permute-done | bytes 1048608 | tf_op jit(solution)/shard_map/ppermute | solution.py:18
  99.6 9.2 %collective-permute-done.10.p_ref = bf16[2,8,128,256]{3,2,1,0:T(8,128)(2,1)S(1)} collective-permute-done((bf16[2,8,128,256]{3,2,1,0:T(8,128)(2,1)}, bf16[2,8,128,256]{3,2,1,0:T(8,128)(2,1)S(1)}, u32[]{:S(2)}, u32[]{:S(2)}) %collective-permute-start.10) | collective-permute-done | bytes 1048608 | tf_op jit(solution)/shard_map/ppermute | solution.py:18
  121.3 43.0 %shard_map.77 = (bf16[2,8,128,256]{3,2,1,0:T(8,128)(2,1)}, bf16[2,8,128,256]{3,2,1,0:T(8,128)(2,1)}, bf16[2,8,128,256]{3,2,1,0:T(8,128)(2,1)}, bf16[2,8,128,256]{3,2,1,0:T(8,128)(2,1)}) custom-call(s32[2,9,32]{2,1,0:T(8,128)} %copy.67.ranks, bf16[2,8192,128]{2,1,0:T(8,128)(2,1)} %refs_9_.3, bf16[2,8192,512]{2,1,0:T(8,128)(2,1)} %col_ref.3, ...), custom_call_target="tpu_custom_call" | custom-call | flops 6442450944 | bytes 29360128 | tf_op jit(solution)/shard_map/pallas_call | solution.py:169
  185.9 9.5 %collective-permute-done.4.p_ref = bf16[2,8,128,256]{3,2,1,0:T(8,128)(2,1)S(1)} collective-permute-done((bf16[2,8,128,256]{3,2,1,0:T(8,128)(2,1)}, bf16[2,8,128,256]{3,2,1,0:T(8,128)(2,1)S(1)}, u32[]{:S(2)}, u32[]{:S(2)}) %collective-permute-start.4) | collective-permute-done | bytes 1048608 | tf_op jit(solution)/shard_map/ppermute | solution.py:18
  207.0 25.9 %all-reduce.11.cloned.1.call-done.sum_ref = bf16[2048,256]{1,0:T(8,128)(2,1)} async-done(((bf16[2048,256]{1,0:T(8,128)(2,1)}), bf16[2048,256]{1,0:T(8,128)(2,1)}) %all-reduce.11.cloned.1.call-update) | async-done | bytes 1048592 | tf_op jit(solution)/shard_map/psum | solution.py:305
  248.9 37.7 %all-reduce.13.cloned.1.call-done.sum_ref = bf16[2048,256]{1,0:T(8,128)(2,1)} async-done(((bf16[2048,256]{1,0:T(8,128)(2,1)}), bf16[2048,256]{1,0:T(8,128)(2,1)}) %all-reduce.13.cloned.1.call-update) | async-done | bytes 1048592 | tf_op jit(solution)/shard_map/psum | solution.py:305
  303.0 37.1 %all-reduce.15.cloned.1.call-done.sum_ref = bf16[2048,256]{1,0:T(8,128)(2,1)} async-done(((bf16[2048,256]{1,0:T(8,128)(2,1)}), bf16[2048,256]{1,0:T(8,128)(2,1)}) %all-reduce.15.cloned.1.call-update) | async-done | bytes 1048592 | tf_op jit(solution)/shard_map/psum | solution.py:305
  357.5 36.7 %all-reduce.17.cloned.1.call-done.sum_ref = bf16[2048,256]{1,0:T(8,128)(2,1)} async-done(((bf16[2048,256]{1,0:T(8,128)(2,1)}), bf16[2048,256]{1,0:T(8,128)(2,1)}) %all-reduce.17.cloned.1.call-update) | async-done | bytes 1048592 | tf_op jit(solution)/shard_map/psum | solution.py:305
  406.1 41.7 %all-reduce.19.cloned.1.call-done.sum_ref = bf16[2048,256]{1,0:T(8,128)(2,1)} async-done(((bf16[2048,256]{1,0:T(8,128)(2,1)}), bf16[2048,256]{1,0:T(8,128)(2,1)}) %all-reduce.19.cloned.1.call-update) | async-done | bytes 1048592 | tf_op jit(solution)/shard_map/psum | solution.py:305
  466.2 5.0 shard_map.97
  476.4 24.9 %all-reduce.21.cloned.1.call-done.sum_ref = bf16[2048,256]{1,0:T(8,128)(2,1)} async-done(((bf16[2048,256]{1,0:T(8,128)(2,1)}), bf16[2048,256]{1,0:T(8,128)(2,1)}) %all-reduce.21.cloned.1.call-update) | async-done | bytes 1048592 | tf_op jit(solution)/shard_map/psum | solution.py:305
  530.8 15.6 %collective-permute-done.42.arr_ref = bf16[2,8,128,256]{3,2,1,0:T(8,128)(2,1)S(1)} collective-permute-done((bf16[2,8,128,256]{3,2,1,0:T(8,128)(2,1)}, bf16[2,8,128,256]{3,2,1,0:T(8,128)(2,1)S(1)}, u32[]{:S(2)}, u32[]{:S(2)}) %collective-permute-start.42) | collective-permute-done | bytes 1048608 | tf_op jit(solution)/shard_map/ppermute | solution.py:18
  547.8 7.2 all-reduce.23.cloned.1.call-done.sum_ref
  560.0 8.9 %collective-permute-done.15.arr_ref = bf16[2,8,128,256]{3,2,1,0:T(8,128)(2,1)} collective-permute-done((bf16[2,8,128,256]{3,2,1,0:T(8,128)(2,1)}, bf16[2,8,128,256]{3,2,1,0:T(8,128)(2,1)}, u32[]{:S(2)}, u32[]{:S(2)}) %collective-permute-start.15) | collective-permute-done | bytes 1048608 | tf_op jit(solution)/shard_map/ppermute | solution.py:18
  584.6 6.8 collective-permute-done.20.arr_ref
  599.7 14.2 %collective-permute-done.25.arr_ref = bf16[2,8,128,256]{3,2,1,0:T(8,128)(2,1)} collective-permute-done((bf16[2,8,128,256]{3,2,1,0:T(8,128)(2,1)}, bf16[2,8,128,256]{3,2,1,0:T(8,128)(2,1)}, u32[]{:S(2)}, u32[]{:S(2)}) %collective-permute-start.25) | collective-permute-done | bytes 1048608 | tf_op jit(solution)/shard_map/ppermute | solution.py:18
  620.0 15.3 %collective-permute-done.30.arr_ref = bf16[2,8,128,256]{3,2,1,0:T(8,128)(2,1)S(1)} collective-permute-done((bf16[2,8,128,256]{3,2,1,0:T(8,128)(2,1)}, bf16[2,8,128,256]{3,2,1,0:T(8,128)(2,1)S(1)}, u32[]{:S(2)}, u32[]{:S(2)}) %collective-permute-start.30) | collective-permute-done | bytes 1048608 | tf_op jit(solution)/shard_map/ppermute | solution.py:18
  657.0 5.5 collective-permute-done.16.arr_ref
  662.5 22.5 %collective-permute-done.21.arr_ref = bf16[2,8,128,256]{3,2,1,0:T(8,128)(2,1)S(1)} collective-permute-done((bf16[2,8,128,256]{3,2,1,0:T(8,128)(2,1)}, bf16[2,8,128,256]{3,2,1,0:T(8,128)(2,1)S(1)}, u32[]{:S(2)}, u32[]{:S(2)}) %collective-permute-start.21) | collective-permute-done | bytes 1048608 | tf_op jit(solution)/shard_map/ppermute | solution.py:18
  689.6 17.8 %collective-permute-done.26.arr_ref = bf16[2,8,128,256]{3,2,1,0:T(8,128)(2,1)S(1)} collective-permute-done((bf16[2,8,128,256]{3,2,1,0:T(8,128)(2,1)}, bf16[2,8,128,256]{3,2,1,0:T(8,128)(2,1)S(1)}, u32[]{:S(2)}, u32[]{:S(2)}) %collective-permute-start.26) | collective-permute-done | bytes 1048608 | tf_op jit(solution)/shard_map/ppermute | solution.py:18
  721.5 5.6 collective-permute-done.31.arr_ref
  734.8 50.0 %shard_map.127.refs_10_ = bf16[2,8192,512]{2,1,0:T(8,128)(2,1)} custom-call(s32[2,9,32]{2,1,0:T(8,128)} %copy.67.ranks, bf16[2,8,128,256]{3,2,1,0:T(8,128)(2,1)} %get-tuple-element.123.refs_0_, bf16[2,8,128,256]{3,2,1,0:T(8,128)(2,1)} %get-tuple-element.128.refs_1_, bf16[2,8,128,256]{3,2,1,0:T(8,128)(2,1)} %get-tuple-element.133.refs_2_, ...), custom_call_target="tpu_custom_call" | custom-call | flops 6442450944 | bytes 41943040 | tf_op jit(solution)/shard_map/pallas_call | solution.py:169
  786.8 50.2 %shard_map.128 = bf16[2,8192,512]{2,1,0:T(8,128)(2,1)} custom-call(s32[2,9,32]{2,1,0:T(8,128)} %copy.67.ranks, bf16[2,8,128,256]{3,2,1,0:T(8,128)(2,1)} %get-tuple-element.90.refs_0_, bf16[2,8,128,256]{3,2,1,0:T(8,128)(2,1)} %get-tuple-element.98.refs_1_, bf16[2,8,128,256]{3,2,1,0:T(8,128)(2,1)} %get-tuple-element.106.refs_2_, ...), custom_call_target="tpu_custom_call", output_to_operand_aliasing={{}: (11, {})} | custom-call | flops 6442450944 | bytes 41943040 | tf_op jit(solution)/shard_map/pallas_call | solution.py:169
  (231 shorter events, 277.2 us)
Async XLA Ops:
  7.2 174.2 %all-reduce.9.cloned.1.call-start = ((), (), s32[]{:S(2)}) async-start(), calls=%async_computation | async-start | bytes 2097152 | tf_op jit(solution)/shard_map/psum | solution.py:305
  93.2 71.1 %collective-permute-start.3 = (bf16[2,8,128,256]{3,2,1,0:T(8,128)(2,1)S(1)}, bf16[2,8,128,256]{3,2,1,0:T(8,128)(2,1)S(1)}, u32[]{:S(2)}, u32[]{:S(2)}) collective-permute-start(bf16[2,8,128,256]{3,2,1,0:T(8,128)(2,1)S(1)} %copy-done.22), channel_id=1, source_target_pairs={{0,1},{1,0},{2,3},{3,2},{4,5},{5,4},{6,7},{7,6},{8,9},{9,8},{10,11... | collective-permute-start | bytes 3145736 | tf_op jit(solution)/shard_map/ppermute | solution.py:18
  98.1 72.5 %collective-permute-start.7 = (bf16[2,8,128,256]{3,2,1,0:T(8,128)(2,1)}, bf16[2,8,128,256]{3,2,1,0:T(8,128)(2,1)S(1)}, u32[]{:S(2)}, u32[]{:S(2)}) collective-permute-start(bf16[2,8,128,256]{3,2,1,0:T(8,128)(2,1)} %shard_map.85.s_ref), channel_id=1, source_target_pairs={{0,2},{1,3},{2,0},{3,1},{4,6},{5,7},{6,4},{7,5},{8,10},{9,11},{10,... | collective-permute-start | bytes 3145736 | tf_op jit(solution)/shard_map/ppermute | solution.py:18
  121.3 111.7 %all-reduce.11.cloned.1.call-start = ((), (), s32[]{:S(2)}) async-start(), calls=%async_computation.1 | async-start | bytes 2097152 | tf_op jit(solution)/shard_map/psum | solution.py:305
  181.4 105.2 %all-reduce.13.cloned.1.call-start = ((), (), s32[]{:S(2)}) async-start(), calls=%async_computation.2 | async-start | bytes 2097152 | tf_op jit(solution)/shard_map/psum | solution.py:305
  232.9 107.2 %all-reduce.15.cloned.1.call-start = ((), (), s32[]{:S(2)}) async-start(), calls=%async_computation.3 | async-start | bytes 2097152 | tf_op jit(solution)/shard_map/psum | solution.py:305
  286.6 107.6 %all-reduce.17.cloned.1.call-start = ((), (), s32[]{:S(2)}) async-start(), calls=%async_computation.4 | async-start | bytes 2097152 | tf_op jit(solution)/shard_map/psum | solution.py:305
  340.1 107.6 %all-reduce.19.cloned.1.call-start = ((), (), s32[]{:S(2)}) async-start(), calls=%async_computation.5 | async-start | bytes 2097152 | tf_op jit(solution)/shard_map/psum | solution.py:305
  394.2 107.2 %all-reduce.21.cloned.1.call-start = ((), (), s32[]{:S(2)}) async-start(), calls=%async_computation.6 | async-start | bytes 2097152 | tf_op jit(solution)/shard_map/psum | solution.py:305
  399.1 72.8 %collective-permute-start.29 = (bf16[2,8,128,256]{3,2,1,0:T(8,128)(2,1)}, bf16[2,8,128,256]{3,2,1,0:T(8,128)(2,1)}, u32[]{:S(2)}, u32[]{:S(2)}) collective-permute-start(bf16[2,8,128,256]{3,2,1,0:T(8,128)(2,1)} %shard_map.114.s_ref), channel_id=1, source_target_pairs={{0,4},{1,5},{2,6},{3,7},{4,0},{5,1},{6,2},{7,3},{8,12},{9,13},{10,... | collective-permute-start | bytes 3145736 | tf_op jit(solution)/shard_map/ppermute | solution.py:18
  447.8 107.3 %all-reduce.23.cloned.1.call-start = ((), (), s32[]{:S(2)}) async-start(), calls=%async_computation.7 | async-start | bytes 2097152 | tf_op jit(solution)/shard_map/psum | solution.py:305
  464.8 65.3 %collective-permute-start.40 = (bf16[2,8,128,256]{3,2,1,0:T(8,128)(2,1)}, bf16[2,8,128,256]{3,2,1,0:T(8,128)(2,1)S(1)}, u32[]{:S(2)}, u32[]{:S(2)}) collective-permute-start(bf16[2,8,128,256]{3,2,1,0:T(8,128)(2,1)} %get-tuple-element.130), channel_id=1, source_target_pairs={{0,4},{1,5},{2,6},{3,7},{4,0},{5,1},{6,2},{7,3},{8,12},{9,13},{10,... | collective-permute-start | bytes 3145736 | tf_op jit(solution)/shard_map/ppermute | solution.py:18
  471.1 75.2 %collective-permute-start.42 = (bf16[2,8,128,256]{3,2,1,0:T(8,128)(2,1)}, bf16[2,8,128,256]{3,2,1,0:T(8,128)(2,1)S(1)}, u32[]{:S(2)}, u32[]{:S(2)}) collective-permute-start(bf16[2,8,128,256]{3,2,1,0:T(8,128)(2,1)} %get-tuple-element.135), channel_id=1, source_target_pairs={{0,4},{1,5},{2,6},{3,7},{4,0},{5,1},{6,2},{7,3},{8,12},{9,13},{10,... | collective-permute-start | bytes 3145736 | tf_op jit(solution)/shard_map/ppermute | solution.py:18
  513.4 84.2 %collective-permute-start.37 = (bf16[2,8,128,256]{3,2,1,0:T(8,128)(2,1)}, bf16[2,8,128,256]{3,2,1,0:T(8,128)(2,1)S(1)}, u32[]{:S(2)}, u32[]{:S(2)}) collective-permute-start(bf16[2,8,128,256]{3,2,1,0:T(8,128)(2,1)} %get-tuple-element.122), channel_id=1, source_target_pairs={{0,2},{1,3},{2,0},{3,1},{4,6},{5,7},{6,4},{7,5},{8,10},{9,11},{10,... | collective-permute-start | bytes 3145736 | tf_op jit(solution)/shard_map/ppermute | solution.py:18
  524.6 66.9 %collective-permute-start.20 = (bf16[2,8,128,256]{3,2,1,0:T(8,128)(2,1)}, bf16[2,8,128,256]{3,2,1,0:T(8,128)(2,1)}, u32[]{:S(2)}, u32[]{:S(2)}) collective-permute-start(bf16[2,8,128,256]{3,2,1,0:T(8,128)(2,1)} %get-tuple-element.95), channel_id=1, source_target_pairs={{0,4},{1,5},{2,6},{3,7},{4,0},{5,1},{6,2},{7,3},{8,12},{9,13},{10,... | collective-permute-start | bytes 3145736 | tf_op jit(solution)/shard_map/ppermute | solution.py:18
  530.1 68.1 %collective-permute-start.39 = (bf16[2,8,128,256]{3,2,1,0:T(8,128)(2,1)}, bf16[2,8,128,256]{3,2,1,0:T(8,128)(2,1)}, u32[]{:S(2)}, u32[]{:S(2)}) collective-permute-start(bf16[2,8,128,256]{3,2,1,0:T(8,128)(2,1)} %get-tuple-element.127), channel_id=1, source_target_pairs={{0,2},{1,3},{2,0},{3,1},{4,6},{5,7},{6,4},{7,5},{8,10},{9,11},{10,... | collective-permute-start | bytes 3145736 | tf_op jit(solution)/shard_map/ppermute | solution.py:18
  546.4 67.5 %collective-permute-start.25 = (bf16[2,8,128,256]{3,2,1,0:T(8,128)(2,1)}, bf16[2,8,128,256]{3,2,1,0:T(8,128)(2,1)}, u32[]{:S(2)}, u32[]{:S(2)}) collective-permute-start(bf16[2,8,128,256]{3,2,1,0:T(8,128)(2,1)} %get-tuple-element.103), channel_id=1, source_target_pairs={{0,4},{1,5},{2,6},{3,7},{4,0},{5,1},{6,2},{7,3},{8,12},{9,13},{10,... | collective-permute-start | bytes 3145736 | tf_op jit(solution)/shard_map/ppermute | solution.py:18
  569.0 66.4 %collective-permute-start.30 = (bf16[2,8,128,256]{3,2,1,0:T(8,128)(2,1)}, bf16[2,8,128,256]{3,2,1,0:T(8,128)(2,1)S(1)}, u32[]{:S(2)}, u32[]{:S(2)}) collective-permute-start(bf16[2,8,128,256]{3,2,1,0:T(8,128)(2,1)} %get-tuple-element.111), channel_id=1, source_target_pairs={{0,4},{1,5},{2,6},{3,7},{4,0},{5,1},{6,2},{7,3},{8,12},{9,13},{10,... | collective-permute-start | bytes 3145736 | tf_op jit(solution)/shard_map/ppermute | solution.py:18
  598.2 64.3 %collective-permute-start.16 = (bf16[2,8,128,256]{3,2,1,0:T(8,128)(2,1)}, bf16[2,8,128,256]{3,2,1,0:T(8,128)(2,1)S(1)}, u32[]{:S(2)}, u32[]{:S(2)}) collective-permute-start(bf16[2,8,128,256]{3,2,1,0:T(8,128)(2,1)} %get-tuple-element.89), channel_id=1, source_target_pairs={{0,2},{1,3},{2,0},{3,1},{4,6},{5,7},{6,4},{7,5},{8,10},{9,11},{10,... | collective-permute-start | bytes 3145736 | tf_op jit(solution)/shard_map/ppermute | solution.py:18
  613.9 71.0 %collective-permute-start.21 = (bf16[2,8,128,256]{3,2,1,0:T(8,128)(2,1)}, bf16[2,8,128,256]{3,2,1,0:T(8,128)(2,1)S(1)}, u32[]{:S(2)}, u32[]{:S(2)}) collective-permute-start(bf16[2,8,128,256]{3,2,1,0:T(8,128)(2,1)} %get-tuple-element.97), channel_id=1, source_target_pairs={{0,2},{1,3},{2,0},{3,1},{4,6},{5,7},{6,4},{7,5},{8,10},{9,11},{10,... | collective-permute-start | bytes 3145736 | tf_op jit(solution)/shard_map/ppermute | solution.py:18
  635.3 72.1 %collective-permute-start.26 = (bf16[2,8,128,256]{3,2,1,0:T(8,128)(2,1)}, bf16[2,8,128,256]{3,2,1,0:T(8,128)(2,1)S(1)}, u32[]{:S(2)}, u32[]{:S(2)}) collective-permute-start(bf16[2,8,128,256]{3,2,1,0:T(8,128)(2,1)} %get-tuple-element.105), channel_id=1, source_target_pairs={{0,2},{1,3},{2,0},{3,1},{4,6},{5,7},{6,4},{7,5},{8,10},{9,11},{10,... | collective-permute-start | bytes 3145736 | tf_op jit(solution)/shard_map/ppermute | solution.py:18
  651.1 76.1 %collective-permute-start.31 = (bf16[2,8,128,256]{3,2,1,0:T(8,128)(2,1)}, bf16[2,8,128,256]{3,2,1,0:T(8,128)(2,1)S(1)}, u32[]{:S(2)}, u32[]{:S(2)}) collective-permute-start(bf16[2,8,128,256]{3,2,1,0:T(8,128)(2,1)} %get-tuple-element.113), channel_id=1, source_target_pairs={{0,2},{1,3},{2,0},{3,1},{4,6},{5,7},{6,4},{7,5},{8,10},{9,11},{10,... | collective-permute-start | bytes 3145736 | tf_op jit(solution)/shard_map/ppermute | solution.py:18
  656.9 75.9 %collective-permute-start.44 = (bf16[2,8,128,256]{3,2,1,0:T(8,128)(2,1)}, bf16[2,8,128,256]{3,2,1,0:T(8,128)(2,1)S(1)}, u32[]{:S(2)}, u32[]{:S(2)}) collective-permute-start(bf16[2,8,128,256]{3,2,1,0:T(8,128)(2,1)} %get-tuple-element.139), channel_id=1, source_target_pairs={{0,1},{1,0},{2,3},{3,2},{4,5},{5,4},{6,7},{7,6},{8,9},{9,8},{10,11... | collective-permute-start | bytes 3145736 | tf_op jit(solution)/shard_map/ppermute | solution.py:18
  662.5 70.4 %collective-permute-start.45 = (bf16[2,8,128,256]{3,2,1,0:T(8,128)(2,1)S(1)}, bf16[2,8,128,256]{3,2,1,0:T(8,128)(2,1)S(1)}, u32[]{:S(2)}, u32[]{:S(2)}) collective-permute-start(bf16[2,8,128,256]{3,2,1,0:T(8,128)(2,1)S(1)} %copy-done.39), channel_id=1, source_target_pairs={{0,1},{1,0},{2,3},{3,2},{4,5},{5,4},{6,7},{7,6},{8,9},{9,8},{10,11... | collective-permute-start | bytes 3145736 | tf_op jit(solution)/shard_map/ppermute | solution.py:18
  (73 other events, 1733.5 us)
Sparse Core Ops, SparseCore 0:
  121.4 52.7 all-reduce.8
  181.5 51.4 all-reduce.10
  235.3 51.1 all-reduce.12
  288.9 51.1 all-reduce.14
  342.9 51.1 all-reduce.16
  396.5 51.1 all-reduce.18
  450.1 51.1 all-reduce.20
  503.8 51.1 all-reduce.22
